TPU v7x, 256 devices: a whole 4x4x8 slice. The times are simulated.
256 devices in a mesh: section: 32 (over x, z), dp: 8 (over y, core).
Axes of the slice: x: 4, y: 4, z: 8, core: 2. Of those that a mesh axis runs over, the one named last changes fastest.
Arguments:
- hidden: bfloat16 [512, 4608], P('dp', 'section'), may hold values from -6 to 6
- norm_gain: float32 [4608], replicated, may hold values from -0.5 to 0.5
- weight: bfloat16 [256000, 4608], P(('section', 'dp'))
- targets: int32 [8, 64], replicated, may hold values from 0 to 255999
- segment_ids: int32 [8, 64], replicated, may hold values from 0 to 7, never falling along the last dimension, each value on 1 to 16 neighbouring positions
- pairing: int32 [8, 8], replicated, may hold values from 0 to 7, each once within a row
- ref_logp: float32 [8, 8], replicated, may hold values from -30 to -20
Outputs:
- hidden_grad: float32 [512, 4608], P('dp', 'section')
- margins: float32 [8, 4], P('dp')
- dpo_loss: float32 [], replicated
Inputs may be any that keep to these rules, and one draw needn't show every extreme that they name: `segment_ids`: within each group's row the segment ids never fall and every one of the 8 segments holds at least one token; one segment of each row holds exactly 16. `pairing`: each row holds every segment number once.
All inputs are finite; a program needn't handle non-finite values.
Results may differ from a plain program's by a relative error of at most 0.0046.
Values may be sent and summed in bfloat16 or wider, within the bound.
A program may use at most 128 MiB of HBM per device.

v0:
```python
import jax
import jax.numpy as jnp
from jax import lax
from jax.sharding import PartitionSpec as P

SOFTCAP = 30.0
DPO_BETA = 0.5
LOSS_SCALE = 65536.0
EPSILON = 1e-06


def dpo_terms(token_logp, segment_ids, pairing, ref_logp):
    num_groups, group_tokens = segment_ids.shape
    seg_count = pairing.shape[1]
    pair_count = seg_count // 2
    logp_rows = token_logp.reshape(num_groups, group_tokens)
    seg_range = jnp.arange(seg_count, dtype=jnp.int32)
    member = (segment_ids[:, :, None] == seg_range[None, None, :]).astype(jnp.float32)
    counts = jnp.sum(member, axis=1)
    seg_mean = jnp.sum(member * logp_rows[:, :, None], axis=1) / counts
    adjusted = seg_mean - ref_logp
    chosen_hot = (pairing[:, 0::2, None] == seg_range[None, None, :]).astype(jnp.float32)
    rejected_hot = (pairing[:, 1::2, None] == seg_range[None, None, :]).astype(jnp.float32)
    chosen = jnp.sum(chosen_hot * adjusted[:, None, :], axis=2)
    rejected = jnp.sum(rejected_hot * adjusted[:, None, :], axis=2)
    margins = DPO_BETA * (chosen - rejected)
    dpo_loss = jnp.mean(jax.nn.softplus(-margins))
    margin_pull = -jax.nn.sigmoid(-margins) * (LOSS_SCALE / (num_groups * pair_count))
    seg_pull = (
        DPO_BETA * jnp.sum((chosen_hot - rejected_hot) * margin_pull[:, :, None], axis=1) / counts
    )
    token_weight = jnp.sum(member * seg_pull[:, None, :], axis=2).reshape(-1)
    return (margins, dpo_loss, token_weight)


def per_device(hidden, norm_gain, weight, targets, segment_ids, pairing, ref_logp):
    section_count = lax.axis_size("section")
    group_count = lax.axis_size("dp")
    section_index = lax.axis_index("section")
    group_index = lax.axis_index("dp")
    group_tokens, col_count = hidden.shape
    model_width = col_count * section_count
    vocab_rows = weight.shape[0]
    gain_scale = 1.0 + norm_gain
    own_scale = lax.dynamic_slice_in_dim(gain_scale, section_index * col_count, col_count)
    hidden32 = hidden.astype(jnp.float32)
    own_squares = jnp.sum(hidden32 * hidden32, axis=1)
    row_squares = lax.psum(own_squares, "section")
    own_inv = lax.rsqrt(row_squares / model_width + EPSILON)
    outgoing = (hidden32 * own_inv[:, None] * own_scale[None, :]).astype(jnp.bfloat16)
    full_rows = lax.all_gather(outgoing, "section", axis=1, tiled=True)
    raw_logits = lax.dot_general(
        weight,
        lax.all_gather(full_rows, "dp", axis=0, tiled=True),
        (((1,), (1,)), ((), ())),
        preferred_element_type=jnp.float32,
    )
    capped = SOFTCAP * jnp.tanh(raw_logits / SOFTCAP)
    vocab_start = (section_index * group_count + group_index) * vocab_rows
    flat_targets = targets.reshape(-1)
    vocab_ids = vocab_start + lax.broadcasted_iota(jnp.int32, (vocab_rows, 1), 0)
    target_hot = vocab_ids == flat_targets[None, :]
    exp_logits = jnp.exp(capped)
    local_total = jnp.sum(exp_logits, axis=0)
    local_pick = jnp.sum(jnp.where(target_hot, capped, 0.0), axis=0)
    exp_total, picked = lax.psum((local_total, local_pick), ("section", "dp"))
    token_logp = picked - jnp.log(exp_total)
    margins, dpo_loss, token_weight = dpo_terms(token_logp, segment_ids, pairing, ref_logp)
    token_prob = exp_logits / exp_total[None, :]
    cap_slope = 1.0 - capped / SOFTCAP * (capped / SOFTCAP)
    dlogit = (
        token_weight[None, :] * (target_hot.astype(jnp.float32) - token_prob) * cap_slope
    ).astype(jnp.bfloat16)
    own_rows = lax.psum_scatter(
        lax.dot_general(
            dlogit, weight, (((0,), (0,)), ((), ())), preferred_element_type=jnp.float32
        ),
        "dp",
        scatter_dimension=0,
        tiled=True,
    )
    grad_normed = lax.psum_scatter(own_rows, "section", scatter_dimension=1, tiled=True)
    dot_part = jnp.sum(grad_normed * own_scale[None, :] * hidden32, axis=1)
    row_dot = lax.psum(dot_part, "section")
    hidden_grad = (
        own_scale[None, :] * own_inv[:, None] * grad_normed
        - hidden32 * (row_dot * own_inv * own_inv * own_inv / model_width)[:, None]
    )
    own_margins = lax.dynamic_slice_in_dim(margins, group_index, 1, 0)
    return (hidden_grad, own_margins, dpo_loss)


def solution(mesh):
    in_specs = (P("dp", "section"), P(), P(("section", "dp"), None), P(), P(), P(), P())
    out_specs = (P("dp", "section"), P("dp", None), P())
    return jax.shard_map(
        per_device, mesh=mesh, in_specs=in_specs, out_specs=out_specs, check_vma=False
    )
```

profile of v0, /device:TPU:8, one launch (start us, length us, event | category | flops | bytes accessed | tf_op | source)
XLA Modules:
  0.0 629.4 jit_solution(11763943927203584538)
XLA Ops:
  7.2 0.9 fusion.14
  8.1 77.7 %psum.28 = f32[64]{0:T(128)S(1)} all-reduce(f32[64]{0:T(128)S(1)} %fusion.14), channel_id=1, replica_groups=mesh['section'=32,'dp'=8] {'section'}, use_global_device_ids=true, to_apply=%region_1.0 | all-reduce | flops 64 | bytes 512 | tf_op jit(solution)/shard_map/psum | solution.py:48
  85.8 0.8 dynamic-slice_add_fusion
  86.5 0.8 fusion.19
  87.4 46.6 %all-gather = bf16[32,144,64]{1,2,0:T(8,128)(2,1)S(1)} all-gather(bf16[1,144,64]{1,2,0:T(8,128)(2,1)S(1)} %fusion.19), channel_id=1, replica_groups=mesh['section'=32,'dp'=8] {'section'}, dimensions={0}, use_global_device_ids=true | all-gather | bytes 608256 | tf_op jit(solution)/shard_map/all_gather | solution.py:51
  134.0 0.6 copy.14
  134.6 2.5 reshape.40
  137.6 33.0 %all-gather.3.cloned.1.call-done = bf16[512,4608]{1,0:T(8,128)(2,1)} async-done(((bf16[64,4608]{1,0:T(8,128)(2,1)}), bf16[512,4608]{1,0:T(8,128)(2,1)}) %all-gather.3.cloned.1.call-update) | async-done | bytes 4718608 | tf_op jit(solution)/shard_map/all_gather | solution.py:54
  170.6 9.4 %fusion = (f32[512]{0:T(512)S(1)}, f32[512]{0:T(512)S(1)}, f32[512,1000]{0,1:T(8,128)S(1)}) fusion(s32[512]{0:T(512)S(1)} %eq.64, s32[1000]{0:T(1024)S(1)} %iota_add_fusion, bf16[512,4608]{1,0:T(8,128)(2,1)} %all-gather.3.cloned.1.call-done, bf16[1000,4608]{1,0:T(8,128)(2,1)} %param.9), kind=kOutput, calls=%fused_computation.2 | convolution fusion | flops 4721662976 | bytes 15992736 | tf_op jit(solution)/shard_map/dot_general | solution.py:52
  180.0 76.9 %all-reduce = (f32[512]{0:T(512)S(1)}, f32[512]{0:T(512)S(1)}) all-reduce(f32[512]{0:T(512)S(1)} %get-tuple-element.7, f32[512]{0:T(512)S(1)} %get-tuple-element.6), channel_id=1, replica_groups=mesh['section'=32,'dp'=8] {'section','dp'}, use_global_device_ids=true, to_apply=%region_5.6 | all-reduce | flops 1024 | bytes 8192 | tf_op jit(solution)/shard_map/psum | solution.py:66
  257.0 0.1 select_reduce_fusion.1
  257.1 0.2 select_reduce_fusion.2
  257.3 0.6 fusion.20
  257.9 0.1 multiply_reduce_fusion
  258.0 0.1 select_reduce_fusion
  258.2 11.5 %fusion.6 = f32[512,4608]{1,0:T(8,128)} fusion(bf16[1000,4608]{1,0:T(8,128)(2,1)} %param.9, f32[512,1000]{0,1:T(8,128)S(1)} %get-tuple-element.16, f32[512]{0:T(512)S(1)} %get-tuple-element.12, f32[512]{0:T(512)S(1)} %mul.186, s32[512]{0:T(512)S(1)} %eq.64, s32[1000]{0:T(1024)S(1)} %iota_add_fusion), kind=kOutput, calls=%fused_computation.10 | convolution fusion | flops 4723712000 | bytes 20711328 | tf_op jit(solution)/shard_map/dot_general | solution.py:75
  269.7 55.0 %reduce-scatter.5.cloned.1.call-done = f32[64,4608]{1,0:T(8,128)} async-done(((f32[512,4608]{1,0:T(8,128)}), f32[64,4608]{1,0:T(8,128)}) %reduce-scatter.5.cloned.1.call-update) | async-done | bytes 1179664 | tf_op jit(solution)/shard_map/reduce_scatter | solution.py:74
  324.7 2.9 copy.16
  327.6 0.6 copy.15
  328.9 218.9 %reduce-scatter.7.cloned.1.call-done = f32[144,64]{1,0:T(8,128)} async-done(((f32[4608,64]{1,0:T(8,128)}), f32[144,64]{1,0:T(8,128)}) %reduce-scatter.7.cloned.1.call-update) | async-done | bytes 36880
  547.7 1.0 copy.17
  548.7 0.1 fusion.17
  548.8 72.2 %psum.31 = f32[64]{0:T(128)S(1)} all-reduce(f32[64]{0:T(128)S(1)} %fusion.17), channel_id=1, replica_groups=mesh['section'=32,'dp'=8] {'section'}, use_global_device_ids=true, to_apply=%region_15.16 | all-reduce | flops 64 | bytes 512 | tf_op jit(solution)/shard_map/psum | solution.py:84
  621.0 0.7 fusion.18
  (31 shorter events, 0.9 us)
Async XLA Ops:
  7.2 163.4 %all-gather.3.cloned.1.call-start = ((), (), s32[]{:S(2)}) async-start(), calls=%async_computation.2 | async-start | bytes 5308416 | tf_op jit(solution)/shard_map/all_gather | solution.py:54
  134.0 3.2 copy-start.1
  134.0 3.4 copy-start.3
  137.1 187.5 %reduce-scatter.5.cloned.1.call-start = ((), (), s32[]{:S(2)}) async-start(), calls=%async_computation.3 | async-start | bytes 10616832 | tf_op jit(solution)/shard_map/reduce_scatter | solution.py:74
  137.6 119.4 %copy-start.2 = (s32[8,64]{1,0:T(8,128)S(1)}, s32[8,64]{1,0:T(8,128)}, u32[]{:S(2)}) copy-start(s32[8,64]{1,0:T(8,128)} %param.11) | copy-start | bytes 6148
  137.6 119.5 %copy-start.4 = (f32[8,8]{1,0:T(8,128)S(1)}, f32[8,8]{1,0:T(8,128)}, u32[]{:S(2)}) copy-start(f32[8,8]{1,0:T(8,128)} %param.13) | copy-start | bytes 772
  269.7 278.1 %reduce-scatter.7.cloned.1.call-start = ((), (), s32[]{:S(2)}) async-start(), calls=%async_computation.4 | async-start | bytes 2433024
  327.5 221.2 %copy-start = (bf16[64,144]{1,0:T(8,128)(2,1)S(1)}, bf16[64,144]{1,0:T(8,128)(2,1)}, u32[]{:S(2)}) copy-start(bf16[64,144]{1,0:T(8,128)(2,1)} %param.7) | copy-start | bytes 55300
Sparse Core Ops, SparseCore 0:
  137.2 33.2 all-gather.2
  269.8 54.8 reduce-scatter.4
  328.5 219.1 reduce-scatter.6
where the time goes:
time: 630 us; the launch traced here: 629 us
  waiting for transfers between devices  307 us (49%)
  blocking collectives  273 us (43%)
  matrix products  20.8 us (3%)
  between operations  15.6 us (2%)
  local copies, waits for them, and re-layouts  8.17 us (1%)
    unnamed x4, waiting for transfers between devices  219 us
    psum x1, blocking collectives, per_device(): row_squares = lax.psum(own_squares, 'section')  77.7 us
    psum x1, blocking collectives, per_device(): exp_total, picked = lax.psum((local_total, local_pick), ('section', 'dp'))  76.9 us
    psum x1, blocking collectives, per_device(): row_dot = lax.psum(dot_part, 'section')  72.2 us
    reduce_scatter x1, waiting for transfers between devices, per_device(): lax.psum_scatter(lax.dot_general(dlogit, weight, (((0,), (0,)), ((), ()))...  55 us
    all_gather x1, blocking collectives, per_device(): full_rows = lax.all_gather(outgoing, 'section', axis=1, tiled=True)  46.6 us
    all_gather x1, waiting for transfers between devices, per_device(): lax.all_gather(full_rows, 'dp', axis=0, tiled=True)  33 us
  transfers between devices with their start and end apart: 3, of which 3 were waited for; matrix products, arithmetic and copies ran while one was open for 0% of the time, Pallas kernels for 0%

commit v1 on v0

v1 whole, which is shorter than its diff:
```python
import jax
import jax.numpy as jnp
from jax import lax
from jax.experimental import pallas as pl
from jax.experimental.pallas import tpu as pltpu
from jax.sharding import PartitionSpec as P

SOFTCAP = 30.0
DPO_BETA = 0.5
LOSS_SCALE = 65536.0
EPSILON = 1e-06
MESH = pl.DeviceIdType.MESH

NX, NY, NZ = 4, 4, 8
D = 4608
BLK = 144
TOK = 512
LANES = 128
VOC = 1000
VPAD = 1024
GROUPS = 8
PAIRS = 4

F32 = jnp.float32
BF16 = jnp.bfloat16

SIZE = {"x": NX, "y": NY, "z": NZ}
AG_ORDER = (("z", "x", "y"), ("z", "y", "x"), ("x", "y", "z"))
RS_ORDER = (("y", "x", "z"), ("x", "y", "z"), ("z", "x", "y"))
PART_ROWS = (32, 32, 16)
PART_AT = (0, 32, 64)


def kernel(
    hidden_ref, gain_ref, w_hbm, tgt_ref, seg_ref, pair_ref, ref_ref,
    out_ref, mar_ref, loss_ref,
    w, wt, wtp, g, n, acc, ebuf, dl, dlp, gainb, hbuf, invs,
    s0, s1, s2, r01, r11, r21, t01, t11, t21, r02, r12, r22, t02, t12, t22, r03, r13, r23,
    fbuf, arz, arx, ary, arc, brz, brx, bry, brc, tbuf, mbuf,
    w_sem, core_send, core_recv, ag_send, ag_recv, fw_send, fw_recv, wt_send, wt_recv, dl_send, dl_recv,
    ar_send, ar_recv, br_send, br_recv, rs_send, rs_recv, fin_send, fin_recv,
):
    sec = lax.axis_index("section")
    grp = lax.axis_index("dp")
    me = {"x": sec // NZ, "z": sec % NZ, "y": grp // 2}
    core = grp % 2
    other = 1 - core

    def device(axis, k):
        at = dict(me)
        at[axis] = lax.rem(me[axis] + k, SIZE[axis])
        return (at["x"] * NZ + at["z"], at["y"] * 2 + core)

    partner = (sec, me["y"] * 2 + other)

    def back(axis, k):
        return lax.rem(me[axis] + (SIZE[axis] - k), SIZE[axis])

    def remote(src, dst, ssem, rsem, dev):
        return pltpu.make_async_remote_copy(
            src_ref=src, dst_ref=dst, send_sem=ssem, recv_sem=rsem, device_id=dev, device_id_type=MESH
        )

    w_copies = [
        pltpu.make_async_copy(
            w_hbm.at[:, pl.ds(x * NZ * BLK, NZ * BLK)], w.at[:, pl.ds(x * NZ * BLK, NZ * BLK)], w_sem.at[x]
        )
        for x in range(NX)
    ]
    for copy in w_copies:
        copy.start()

    barrier = pltpu.get_barrier_semaphore()
    pl.semaphore_signal(barrier, inc=1, device_id=partner, device_id_type=MESH)
    for axis in "xyz":
        for k in range(1, SIZE[axis]):
            pl.semaphore_signal(barrier, inc=1, device_id=device(axis, k), device_id_type=MESH)
    pl.semaphore_wait(barrier, 1 + NX + NY + NZ - 3)

    swap = remote(hidden_ref, hbuf.at[core], core_send, core_recv, partner)
    swap.start()
    hbuf[core] = hidden_ref[...]
    swap.wait()
    both = jnp.concatenate([hbuf[0], hbuf[1]], axis=0).astype(F32)
    both = jnp.concatenate([both, jnp.zeros((LANES, 2 * LANES - BLK), F32)], axis=1)
    own_block = jnp.transpose(both)[:BLK]
    own_block = own_block.astype(BF16)
    own_at = pl.multiple_of(80 * core, 16)
    g[me["y"], me["x"], me["z"], pl.ds(own_at, 64), :] = jnp.where(core == 0, own_block[0:64], own_block[80:144])
    g[me["y"], me["x"], me["z"], 64:80, :] = own_block[64:80]

    part_at = (80 * core, 80 * core + 32, 64)

    def g_slice(part, at):
        row = part_at[part]
        if part < 2:
            row = pl.multiple_of(row, 16)
        idx = [pl.ds(0, SIZE[a]) if at[a] is None else at[a] for a in ("y", "x", "z")]
        return g.at[idx[0], idx[1], idx[2], pl.ds(row, PART_ROWS[part]), :]

    def ag_stage(part, stage):
        axis = AG_ORDER[part][stage]
        at = dict(me)
        for done in AG_ORDER[part][:stage]:
            at[done] = None
        copies = []
        for k in range(1, SIZE[axis]):
            piece = g_slice(part, at)
            copies.append(
                remote(piece, piece, ag_send.at[part, stage, k], ag_recv.at[part, stage, k], device(axis, k))
            )
        return copies

    def forward(part, k):
        axis = AG_ORDER[part][2]
        at = {a: None for a in "xyz"}
        at[axis] = back(axis, k)
        piece = g_slice(part, at)
        return remote(piece, piece, fw_send.at[part, k], fw_recv.at[part, k], partner)

    def transpose_weight(x):
        w_copies[x].wait()
        for i in range(NZ * BLK // LANES):
            cols = w[:, pl.ds(x * NZ * BLK + i * LANES, LANES)].astype(F32)
            cols = jnp.concatenate([cols, jnp.zeros((VPAD - VOC, LANES), F32)], axis=0)
            flipped = jnp.transpose(cols).astype(BF16)
            row = i * LANES
            while row < (i + 1) * LANES:
                z, off = row // BLK, row % BLK
                count = min(BLK - off, (i + 1) * LANES - row)
                wt[x, z, off:off + count, :] = flipped[row - i * LANES:row - i * LANES + count]
                row += count

    def gain_rows(i, carry):
        row = 1.0 + gain_ref[pl.ds(i, 1), :]
        gainb[pl.ds(pl.multiple_of(i * LANES, LANES), LANES), :] = jnp.transpose(
            jnp.broadcast_to(row, (LANES, LANES))
        )
        return carry

    copies = [[ag_stage(p, s) for s in range(3)] for p in range(3)]
    for p in range(3):
        for c in copies[p][0]:
            c.start()
    transpose_weight(0)
    for s in range(1, 3):
        for p in range(3):
            for c in copies[p][s - 1]:
                c.wait()
            for c in copies[p][s]:
                c.start()
        if s == 1:
            transpose_weight(1)
    forwards = []
    for p in range(2):
        f = forward(p, 0)
        f.start()
        forwards.append(f)
    transpose_weight(2)
    for k in (0, 2, 1):
        for p in range(2):
            copies[p][2][k].wait()
            f = forward(p, k + 1)
            f.start()
            forwards.append(f)
    transpose_weight(3)
    lax.fori_loop(0, D // LANES, gain_rows, 0)
    for c in copies[2][2]:
        c.wait()
    for f in forwards:
        f.wait()

    far = pl.multiple_of(80 * other, 16)
    wt_copies = [
        remote(wt.at[:, :, pl.ds(far, 64), :], wtp.at[:, :, pl.ds(0, 64), :], wt_send.at[0], wt_recv.at[0], partner),
        remote(wt.at[:, :, pl.ds(64, 16), :], wtp.at[:, :, pl.ds(64, 16), :], wt_send.at[1], wt_recv.at[1], partner),
    ]
    for c in wt_copies:
        c.start()

    def squares(i, sums):
        x, z = i // NZ, i % NZ
        res = []
        for y in range(NY):
            h = g[y, x, z].astype(F32)
            res.append(sums[y] + jnp.sum((h * h).reshape(BLK // 8, 8, LANES), axis=0))
        return tuple(res)

    sums = lax.fori_loop(0, NX * NZ, squares, tuple(jnp.zeros((8, LANES), F32) for _ in range(NY)))
    mean_sq = jnp.concatenate([jnp.sum(v, axis=0, keepdims=True) for v in sums], axis=0) / D
    inv = lax.rsqrt(mean_sq + EPSILON)
    invs[0:NY, :] = inv

    def normalize(i, carry):
        x, z = i // NZ, i % NZ
        rows = pl.ds(pl.multiple_of(i * BLK, BLK), BLK)
        gain = gainb[rows, :]
        for y in range(NY):
            h = g[y, x, z].astype(F32)
            n[rows, y * LANES:(y + 1) * LANES] = (h * inv[y:y + 1] * gain).astype(BF16)
        return carry

    lax.fori_loop(0, NX * NZ, normalize, 0)

    depth = 256
    acc[0:VOC, :] = jnp.dot(w[:, 0:depth], n[0:depth, :], preferred_element_type=F32)

    def logits(i, carry):
        at = pl.ds(pl.multiple_of(i * depth, depth), depth)
        acc[0:VOC, :] += jnp.dot(w[:, at], n[at, :], preferred_element_type=F32)
        return carry

    lax.fori_loop(1, D // depth, logits, 0)

    tile = 128
    vocab_start = (sec * 2 * NY + grp) * VOC
    targets = tgt_ref[...]

    def row_ids(i):
        return i * tile + lax.broadcasted_iota(jnp.int32, (tile, TOK), 0)

    def fold(v):
        return jnp.sum(v.reshape(tile // 8, 8, TOK), axis=0)

    def softmax_tile(i, carry):
        tot, pick = carry
        at = pl.ds(pl.multiple_of(i * tile, tile), tile)
        ids = row_ids(i)
        valid = ids < VOC
        capped = SOFTCAP * jnp.tanh(acc[at, :] * (1.0 / SOFTCAP))
        e = jnp.where(valid, jnp.exp(capped), 0.0)
        ebuf[at, :] = e
        hot = jnp.logical_and(ids + vocab_start == targets, valid)
        return (tot + fold(e), pick + fold(jnp.where(hot, capped, 0.0)))

    zero = jnp.zeros((8, TOK), F32)
    tot, pick = lax.fori_loop(0, VPAD // tile, softmax_tile, (zero, zero))

    def to_rows(v):
        v = jnp.sum(v, axis=0, keepdims=True)
        return [v[:, y * LANES:(y + 1) * LANES] for y in range(NY)]

    def reduce_copies(buf, axis, ssem, rsem, stage):
        if axis == "c":
            piece = buf.at[core]
            return [remote(piece, piece, ssem.at[stage, 0], rsem.at[stage, 0], partner)]
        piece = buf.at[me[axis]]
        return [
            remote(piece, piece, ssem.at[stage, k], rsem.at[stage, k], device(axis, k)) for k in range(1, SIZE[axis])
        ]

    def reduce_start(value, buf, axis, ssem, rsem, stage):
        buf[core if axis == "c" else me[axis]] = value
        cs = reduce_copies(buf, axis, ssem, rsem, stage)
        for c in cs:
            c.start()
        return cs

    def reduce_end(cs, buf):
        for c in cs:
            c.wait()
        return jnp.sum(buf[...], axis=0)

    value = jnp.concatenate(to_rows(tot) + to_rows(pick), axis=0)
    for stage, (axis, buf) in enumerate((("z", arz), ("x", arx), ("y", ary), ("c", arc))):
        value = reduce_end(reduce_start(value, buf, axis, ar_send, ar_recv, stage), buf)

    exp_total = value[0:NY]
    logp = value[NY:2 * NY] - jnp.log(exp_total)

    def twice(v):
        return jnp.concatenate([v[r // 2:r // 2 + 1] for r in range(GROUPS)], axis=0)

    lane = lax.broadcasted_iota(jnp.int32, (GROUPS, LANES), 1)
    group = lax.broadcasted_iota(jnp.int32, (GROUPS, LANES), 0)
    own_half = (lane // 64) == (group % 2)
    seg = jnp.where(own_half, twice(seg_ref[...]), -1)
    logp = twice(logp)
    pairing = pair_ref[...]
    ref_logp = ref_ref[...]
    members, counts, adjusted = [], [], []
    for s in range(GROUPS):
        member = (seg == s).astype(F32)
        count = jnp.sum(member, axis=1, keepdims=True)
        members.append(member)
        counts.append(count)
        adjusted.append(jnp.sum(member * logp, axis=1, keepdims=True) / count - ref_logp[:, s:s + 1])
    margins, pulls, hots = [], [], []
    loss = jnp.zeros((GROUPS, 1), F32)
    for k in range(PAIRS):
        signs = [
            (pairing[:, 2 * k:2 * k + 1] == s).astype(F32) - (pairing[:, 2 * k + 1:2 * k + 2] == s).astype(F32)
            for s in range(GROUPS)
        ]
        margin = DPO_BETA * sum(sign * a for sign, a in zip(signs, adjusted))
        loss = loss + jnp.maximum(-margin, 0.0) + jnp.log1p(jnp.exp(-jnp.abs(margin)))
        hots.append(signs)
        margins.append(margin)
        pulls.append(-jax.nn.sigmoid(-margin) * (LOSS_SCALE / (GROUPS * PAIRS)))
    weight_rows = jnp.zeros((GROUPS, LANES), F32)
    for s in range(GROUPS):
        pull = DPO_BETA * sum(hots[k][s] * pulls[k] for k in range(PAIRS)) / counts[s]
        weight_rows = weight_rows + members[s] * pull
    token_weight = jnp.concatenate(
        [weight_rows[2 * y:2 * y + 1] + weight_rows[2 * y + 1:2 * y + 2] for y in range(NY)], axis=1
    )
    inv_total = 1.0 / exp_total
    inv_total = jnp.concatenate([inv_total[y:y + 1] for y in range(NY)], axis=1)

    def grad_tile(i, row_dot):
        at = pl.ds(pl.multiple_of(i * tile, tile), tile)
        ids = row_ids(i)
        valid = ids < VOC
        raw = acc[at, :]
        th = jnp.tanh(raw * (1.0 / SOFTCAP))
        hot = (ids + vocab_start == targets).astype(F32)
        d = token_weight * (hot - ebuf[at, :] * inv_total) * (1.0 - th * th)
        d = jnp.where(valid, d, 0.0).astype(BF16)
        dl[at, :] = d
        d = d.astype(F32)
        return row_dot + fold(jnp.where(d == 0.0, 0.0, d * raw))

    row_dot = zero
    dl_copies = []
    for q in range(4):
        row_dot = lax.fori_loop(2 * q, 2 * q + 2, grad_tile, row_dot)
        at = pl.ds(q * 2 * tile, 2 * tile)
        c = remote(dl.at[at, :], dlp.at[at, :], dl_send.at[q], dl_recv.at[q], partner)
        c.start()
        dl_copies.append(c)

    br_value = jnp.concatenate(to_rows(row_dot) + [jnp.zeros((NY, LANES), F32)], axis=0)
    br_copies = reduce_start(br_value, brz, "z", br_send, br_recv, 0)

    col = lax.broadcasted_iota(jnp.int32, (GROUPS, LANES), 1)
    mbuf[...] = sum(jnp.where(col == k, margins[k], 0.0) for k in range(PAIRS))
    mar_ref[...] = mbuf[pl.ds(grp, 1), :][:, 0:PAIRS]
    loss_ref[...] = jnp.sum(loss, axis=0, keepdims=True) * (1.0 / (GROUPS * PAIRS))

    for c in wt_copies:
        c.wait()
    for c in dl_copies:
        c.wait()

    def terms(part, xs, s):
        rows = PART_ROWS[part]
        near = part_at[part] if part == 2 else pl.multiple_of(part_at[part], 16)

        def body(i, carry):
            a = wt[pl.ds(i * xs, xs), :, pl.ds(near, rows), :].reshape(xs * NZ * rows, VPAD)
            b = wtp[pl.ds(i * xs, xs), :, pl.ds(PART_AT[part], rows), :].reshape(xs * NZ * rows, VPAD)
            t = jnp.dot(a, dl[...], preferred_element_type=F32)
            t = t + jnp.dot(b, dlp[...], preferred_element_type=F32)
            t = t.astype(BF16)
            for y in range(NY):
                s[y, pl.ds(i * xs, xs)] = t[:, y * LANES:(y + 1) * LANES].reshape(xs, NZ, rows, LANES)
            return carry

        lax.fori_loop(0, NX // xs, body, 0)

    def scatter(part, stage, src, dst):
        axis = RS_ORDER[part][stage]
        cs = []
        for k in range(1, SIZE[axis]):
            to = lax.rem(me[axis] + k, SIZE[axis])
            cs.append(
                remote(src(to), dst.at[me[axis]], rs_send.at[part, stage, k], rs_recv.at[part, stage, k], device(axis, k))
            )
        for c in cs:
            c.start()
        return cs

    def total(part, stage, cs, own, dst):
        axis = RS_ORDER[part][stage]
        for c in cs:
            c.wait()
        return [own] + [dst.at[back(axis, k)] for k in range(1, SIZE[axis])]

    def add_up(refs, lead, out):
        def body(i, carry):
            v = refs[0][i].astype(F32)
            for r in refs[1:]:
                v = v + r[i].astype(F32)
            out[i] = v.astype(BF16)
            return carry

        lax.fori_loop(0, lead, body, 0)

    terms(2, 4, s2)
    c2 = scatter(2, 0, lambda to: s2.at[:, :, to], r21)
    terms(0, 2, s0)
    c0 = scatter(0, 0, lambda to: s0.at[to], r01)
    terms(1, 2, s1)
    c1 = scatter(1, 0, lambda to: s1.at[:, to], r11)

    br_value = reduce_end(br_copies, brz)
    br_copies = reduce_start(br_value, brx, "x", br_send, br_recv, 1)

    add_up(total(1, 0, c1, s1.at[:, me["x"]], r11), NY, t11)
    c1 = scatter(1, 1, lambda to: t11.at[to], r12)
    br_value = reduce_end(br_copies, brx)
    br_copies = reduce_start(br_value, bry, "y", br_send, br_recv, 2)
    add_up(total(0, 0, c0, s0.at[me["y"]], r01), NX, t01)
    c0 = scatter(0, 1, lambda to: t01.at[to], r02)
    add_up(total(2, 0, c2, s2.at[:, :, me["z"]], r21), NY, t21)
    c2 = scatter(2, 1, lambda to: t21.at[:, to], r22)
    br_value = reduce_end(br_copies, bry)
    br_copies = reduce_start(br_value, brc, "c", br_send, br_recv, 3)

    add_up(total(1, 1, c1, t11.at[me["y"]], r12), NZ, t12)
    c1 = scatter(1, 2, lambda to: t12.at[to], r13)
    add_up(total(0, 1, c0, t01.at[me["x"]], r02), NZ, t02)
    c0 = scatter(0, 2, lambda to: t02.at[to], r03)
    add_up(total(2, 1, c2, t21.at[:, me["x"]], r22), NY, t22)
    c2 = scatter(2, 2, lambda to: t22.at[to], r23)
    row_dot = reduce_end(br_copies, brc)
    tbuf[0:8, :] = row_dot

    def last(refs):
        v = refs[0][...].astype(F32)
        for r in refs[1:]:
            v = v + r[...].astype(F32)
        return v

    fbuf[pl.ds(64, 16), :] = last(total(2, 2, c2, t22.at[me["y"]], r23))
    fbuf[pl.ds(pl.multiple_of(80 * core, 16), 32), :] = last(total(0, 2, c0, t02.at[me["z"]], r03))
    fbuf[pl.ds(pl.multiple_of(80 * core + 32, 16), 32), :] = last(total(1, 2, c1, t12.at[me["z"]], r13))
    mine = fbuf.at[pl.ds(pl.multiple_of(80 * core, 16), 64), :]
    swap = remote(mine, mine, fin_send, fin_recv, partner)
    swap.start()
    swap.wait()

    own_inv = invs[pl.ds(me["y"], 1), :]
    own_dot = tbuf[pl.ds(me["y"], 1), :]
    own_gain = gainb[pl.ds(pl.multiple_of(sec * BLK, BLK), BLK), :]
    own_hidden = g[me["y"], me["x"], me["z"]].astype(F32)
    result = own_gain * own_inv * fbuf[...] - own_hidden * (own_dot * own_inv * own_inv * (1.0 / D))
    result = jnp.concatenate([result, jnp.zeros((2 * LANES - BLK, LANES), F32)], axis=0)
    flipped = jnp.transpose(result)
    out_ref[...] = jnp.where(core == 0, flipped[0:64, 0:BLK], flipped[64:128, 0:BLK])


def per_device(hidden, norm_gain, weight, targets, segment_ids, pairing, ref_logp):
    vmem = pl.BlockSpec(memory_space=pltpu.VMEM)
    dma = pltpu.SemaphoreType.DMA
    V = pltpu.VMEM
    grad, margins, loss = pl.pallas_call(
        kernel,
        out_shape=(
            jax.ShapeDtypeStruct((64, BLK), F32),
            jax.ShapeDtypeStruct((1, PAIRS), F32),
            jax.ShapeDtypeStruct((1, 1), F32),
        ),
        in_specs=[vmem, vmem, pl.BlockSpec(memory_space=pl.ANY), vmem, vmem, vmem, vmem],
        out_specs=(vmem, vmem, vmem),
        scratch_shapes=[
            V((VOC, D), BF16),
            V((NX, NZ, BLK, VPAD), BF16),
            V((NX, NZ, 80, VPAD), BF16),
            V((NY, NX, NZ, BLK, LANES), BF16),
            V((D, TOK), BF16),
            V((VPAD, TOK), F32),
            V((VPAD, TOK), F32),
            V((VPAD, TOK), BF16),
            V((VPAD, TOK), BF16),
            V((D, LANES), F32),
            V((2, 64, BLK), BF16),
            V((8, LANES), F32),
            V((NY, NX, NZ, 32, LANES), BF16),
            V((NY, NX, NZ, 32, LANES), BF16),
            V((NY, NX, NZ, 16, LANES), BF16),
            V((NY, NX, NZ, 32, LANES), BF16),
            V((NX, NY, NZ, 32, LANES), BF16),
            V((NZ, NY, NX, 16, LANES), BF16),
            V((NX, NZ, 32, LANES), BF16),
            V((NY, NZ, 32, LANES), BF16),
            V((NY, NX, 16, LANES), BF16),
            V((NX, NZ, 32, LANES), BF16),
            V((NY, NZ, 32, LANES), BF16),
            V((NX, NY, 16, LANES), BF16),
            V((NZ, 32, LANES), BF16),
            V((NZ, 32, LANES), BF16),
            V((NY, 16, LANES), BF16),
            V((NZ, 32, LANES), BF16),
            V((NZ, 32, LANES), BF16),
            V((NY, 16, LANES), BF16),
            V((BLK, LANES), F32),
            V((NZ, 8, LANES), F32),
            V((NX, 8, LANES), F32),
            V((NY, 8, LANES), F32),
            V((2, 8, LANES), F32),
            V((NZ, 8, LANES), F32),
            V((NX, 8, LANES), F32),
            V((NY, 8, LANES), F32),
            V((2, 8, LANES), F32),
            V((8, LANES), F32),
            V((8, LANES), F32),
            dma((NX,)),
            dma, dma,
            dma((3, 3, NZ)), dma((3, 3, NZ)),
            dma((2, 4)), dma((2, 4)),
            dma((2,)), dma((2,)),
            dma((4,)), dma((4,)),
            dma((4, NZ)), dma((4, NZ)),
            dma((4, NZ)), dma((4, NZ)),
            dma((3, 3, NZ)), dma((3, 3, NZ)),
            dma, dma,
        ],
        compiler_params=pltpu.CompilerParams(
            collective_id=0, has_side_effects=True, vmem_limit_bytes=60 * 2**20
        ),
        name="dpo_output_layer",
    )(
        hidden,
        norm_gain.reshape(D // LANES, LANES),
        weight,
        targets.reshape(1, TOK),
        segment_ids.reshape(NY, LANES),
        pairing,
        ref_logp,
    )
    return (grad, margins, loss.reshape(()))


def solution(mesh):
    in_specs = (P("dp", "section"), P(), P(("section", "dp"), None), P(), P(), P(), P())
    out_specs = (P("dp", "section"), P("dp", None), P())
    return jax.shard_map(
        per_device, mesh=mesh, in_specs=in_specs, out_specs=out_specs, check_vma=False
    )
```

time: 630 us -> 113 us (0.18)
  the two profiles are of different devices: /device:TPU:8 before, /device:TPU:1 now
where the time goes in v1:
time: 113 us; the launch traced here: 112 us
  Pallas kernels  105 us (93%)
  local copies, waits for them, and re-layouts  5.25 us (5%)
  between operations  2.46 us (2%)
    pallas_call x1, Pallas kernels, per_device(): pl.pallas_call(kernel, out_shape=(jax.ShapeDtypeStruct((64, BLK), F32), j...  105 us
    unnamed x2, local copies, waits for them, and re-layouts  2.58 us

profile of v1, /device:TPU:1, one launch (start us, length us, event | category | flops | bytes accessed | tf_op | source)
XLA Modules:
  0.0 112.4 jit_solution(5584538952451595780)
XLA Ops:
  0.6 1.3 %reshape.19.tgt_ref = s32[1,512]{1,0:T(1,128)} reshape(s32[8,64]{1,0:T(8,128)} %param.10) | data formatting | bytes 4096 | tf_op jit(solution)/shard_map/reshape | solution.py:517
  2.0 1.3 %reshape.20.seg_ref = s32[4,128]{1,0:T(4,128)} reshape(s32[8,64]{1,0:T(8,128)} %param.11) | data formatting | bytes 4096 | tf_op jit(solution)/shard_map/reshape | solution.py:518
  3.3 104.7 %dpo_output_layer.1 = (f32[64,144]{1,0:T(8,128)}, f32[1,4]{1,0:T(1,128)}, f32[1,1]{1,0:T(1,128)}) custom-call(bf16[64,144]{1,0:T(8,128)(2,1)} %hidden_ref.1, f32[36,128]{1,0:T(8,128)} %bitcast.2, bf16[1000,4608]{1,0:T(8,128)(2,1)} %w_hbm.1, s32[1,512]{1,0:T(1,128)} %reshape.19.tgt_ref, s32[4,128]{1,0:T(4,128)} %reshape.20.seg_ref, s32[8,8]{1,0:T(8,128)} %pair_ref.1, ...), custom_call_target="tpu_custom_call" | custom-call | tf_op jit(solution)/shard_map/dpo_output_layer/pallas_call | solution.py:447
  108.0 1.5 %copy.13 = f32[64,144]{1,0:T(8,128)} copy(f32[64,144]{1,0:T(8,128)} %get-tuple-element.12) | data formatting | bytes 73728
  109.5 1.1 copy.14

commit v2 on v0

v2 whole, which is shorter than its diff:
```python
import jax
import jax.numpy as jnp
from jax import lax
from jax.experimental import pallas as pl
from jax.experimental.pallas import tpu as pltpu
from jax.sharding import PartitionSpec as P

SOFTCAP = 30.0
DPO_BETA = 0.5
LOSS_SCALE = 65536.0
EPSILON = 1e-06
MESH = pl.DeviceIdType.MESH

NX, NY, NZ = 4, 4, 8
D = 4608
BLK = 144
TOK = 512
LANES = 128
VOC = 1000
VPAD = 1024
V_ALL = 256000
GROUPS = 8
PAIRS = 4

F32 = jnp.float32
BF16 = jnp.bfloat16

SIZE = {"x": NX, "y": NY, "z": NZ}
AG_ORDER = (("z", "x", "y"), ("z", "y", "x"), ("y", "x", "z"))
OWN = 64
MID = 16
RS_ORDER = (("y", "x", "z"), ("x", "y", "z"), ("z", "x", "y"))
PART_ROWS = (32, 32, 16)
PART_AT = (0, 32, 64)


def kernel(
    hid_hbm, gain_hbm, w_hbm, tgt_hbm, seg_hbm, pair_hbm, ref_hbm,
    out_ref, mar_ref, loss_ref,
    gain_ref, tgt_ref, seg_ref, pair_ref, ref_ref,
    w, wt, wtp, g, n, acc, hot, hotp, dl, dlp, gainb, hbuf, invs,
    u0, u1, u2, a0, a1, a2,
    s0, s1, s2, r01, r11, r21, t01, t11, t21, r02, r12, r22, t02, t12, t22, r03, r13, r23,
    fbuf, arz, arx, ary, arc, sqz, sqx, sqy, coef, dotb, mbuf,
    in_sem, w_sem, core_send, core_recv, ag1_send, ag1_recv, ag2_send, ag2_recv, ag3_send, ag3_recv, fw_send, fw_recv,
    wt_send, wt_recv, dl_send, dl_recv, ar_send, ar_recv, sq_send, sq_recv,
    rs1_send, rs1_recv, rs2_send, rs2_recv, rs3_send, rs3_recv, fin_send, fin_recv,
):
    sec = lax.axis_index("section")
    grp = lax.axis_index("dp")
    me = {"x": sec // NZ, "z": sec % NZ, "y": grp // 2}
    core = grp % 2
    other = 1 - core

    def device(axis, k):
        at = dict(me)
        at[axis] = ahead(axis, k)
        return (at["x"] * NZ + at["z"], at["y"] * 2 + core)

    partner = (sec, me["y"] * 2 + other)

    def ahead(axis, k):
        return lax.rem(me[axis] + k, SIZE[axis])

    def back(axis, k):
        return lax.rem(me[axis] + (SIZE[axis] - k), SIZE[axis])

    def remote(src, dst, ssem, rsem, dev):
        return pltpu.make_async_remote_copy(
            src_ref=src, dst_ref=dst, send_sem=ssem, recv_sem=rsem, device_id=dev, device_id_type=MESH
        )

    def start(copies):
        for c in copies:
            c.start()
        return copies

    def wait(copies):
        for c in copies:
            c.wait()

    cut = NZ * BLK
    small = ((hid_hbm, hbuf.at[core]), (gain_hbm, gain_ref), (tgt_hbm, tgt_ref), (seg_hbm, seg_ref),
             (pair_hbm, pair_ref), (ref_hbm, ref_ref))
    in_copies = start([pltpu.make_async_copy(src, dst, in_sem.at[i]) for i, (src, dst) in enumerate(small)])
    w_copies = start([
        pltpu.make_async_copy(w_hbm.at[:, pl.ds(x * cut, cut)], w.at[:, pl.ds(x * cut, cut)], w_sem.at[x])
        for x in range(NX)
    ])

    barrier = pltpu.get_barrier_semaphore()
    pl.semaphore_signal(barrier, inc=1, device_id=partner, device_id_type=MESH)
    for axis in "xyz":
        for k in range(1, SIZE[axis]):
            pl.semaphore_signal(barrier, inc=1, device_id=device(axis, k), device_id_type=MESH)
    pl.semaphore_wait(barrier, 1 + NX + NY + NZ - 3)

    in_copies[0].wait()
    swap = remote(hbuf.at[core], hbuf.at[core], core_send, core_recv, partner)
    swap.start()
    wait(in_copies[1:])
    swap.wait()
    both = jnp.concatenate([hbuf[0], hbuf[1]], axis=0).astype(F32)
    both = jnp.concatenate([both, jnp.zeros((LANES, 2 * LANES - BLK), F32)], axis=1)
    own_block = jnp.transpose(both)[:BLK]
    own_bits = own_block.astype(BF16)
    own_at = pl.multiple_of(80 * core, 16)
    g[me["y"], me["x"], me["z"], pl.ds(own_at, 64), :] = jnp.where(core == 0, own_bits[0:64], own_bits[80:144])
    g[me["y"], me["x"], me["z"], 64:80, :] = own_bits[64:80]

    part_at = (own_at, pl.multiple_of(80 * core + 32, 16), OWN)

    def g_slice(at, row, rows):
        idx = [at[a] if a in at else pl.ds(0, SIZE[a]) for a in ("y", "x", "z")]
        return g.at[idx[0], idx[1], idx[2], pl.ds(row, rows), :]

    def ag_first(i, axis, row, rows):
        piece = g_slice(me, row, rows)
        return [
            remote(piece, piece, ag1_send.at[i, k], ag1_recv.at[i, k], device(axis, k)) for k in range(1, SIZE[axis])
        ]

    def ag_second(part):
        first, axis, _ = AG_ORDER[part]
        piece = g_slice({a: me[a] for a in me if a != first}, part_at[part], PART_ROWS[part])
        return [
            remote(piece, piece, ag2_send.at[part, k], ag2_recv.at[part, k], device(axis, k)) for k in range(1, 4)
        ]

    def ag_last(part, j):
        _, second, third = AG_ORDER[part]
        piece = g_slice({second: back(second, j), third: me[third]}, part_at[part], PART_ROWS[part])
        return [
            remote(piece, piece, ag3_send.at[part, j, k], ag3_recv.at[part, j, k], device(third, k))
            for k in range(1, SIZE[third])
        ]

    forwards = {}

    def forward(part, j, k):
        _, second, third = AG_ORDER[part]
        piece = g_slice({second: back(second, j), third: back(third, k)}, part_at[part], PART_ROWS[part])
        c = remote(piece, piece, fw_send.at[part, j, k], fw_recv.at[part, j, k], partner)
        c.start()
        forwards[part, j, k] = c

    def sum_copies(buf, axis, ssem, rsem, stage):
        if axis == "c":
            piece = buf.at[core]
            return [remote(piece, piece, ssem.at[stage, 0], rsem.at[stage, 0], partner)]
        piece = buf.at[me[axis]]
        return [
            remote(piece, piece, ssem.at[stage, k], rsem.at[stage, k], device(axis, k)) for k in range(1, SIZE[axis])
        ]

    def sum_start(value, buf, axis, ssem, rsem, stage):
        buf[core if axis == "c" else me[axis]] = value
        return start(sum_copies(buf, axis, ssem, rsem, stage))

    def sum_end(copies, buf):
        wait(copies)
        return jnp.sum(buf[...], axis=0)

    stage1 = start(ag_first(0, "z", own_at, OWN))
    mid1 = start(ag_first(1, "y", OWN, MID))
    squares = jnp.sum((own_block * own_block).reshape(BLK // 8, 8, LANES), axis=0)
    sq = sum_start(squares, sqz, "z", sq_send, sq_recv, 0)

    def transpose_weight(x):
        w_copies[x].wait()
        for i in range(cut // LANES):
            cols = w[:, pl.ds(x * cut + i * LANES, LANES)].astype(F32)
            cols = jnp.concatenate([cols, jnp.zeros((VPAD - VOC, LANES), F32)], axis=0)
            flipped = jnp.transpose(cols).astype(BF16)
            row = i * LANES
            while row < (i + 1) * LANES:
                z, off = row // BLK, row % BLK
                count = min(BLK - off, (i + 1) * LANES - row)
                wt[x, z, off:off + count, :] = flipped[row - i * LANES:row - i * LANES + count]
                row += count

    def gain_rows(i, carry):
        for q in range(4):
            row = 1.0 + gain_ref[pl.ds(4 * i + q, 1), :]
            gainb[pl.ds(pl.multiple_of((4 * i + q) * LANES, LANES), LANES), :] = jnp.transpose(
                jnp.broadcast_to(row, (LANES, LANES))
            )
        return carry

    stage2, stage3 = {}, {}

    def first_done(p):
        stage2[p] = start(ag_second(p))
        stage3[p, 0] = start(ag_last(p, 0))
        if p < 2:
            forward(p, 0, 0)

    transpose_weight(0)
    transpose_weight(1)
    wait(mid1)
    first_done(2)
    transpose_weight(2)
    transpose_weight(3)
    wait(stage1)
    first_done(0)
    first_done(1)
    sq = sum_start(sum_end(sq, sqz), sqx, "x", sq_send, sq_recv, 1)

    tile = 128
    vocab_start = (sec * 2 * NY + grp) * VOC
    other_start = (sec * 2 * NY + me["y"] * 2 + other) * VOC
    half = lax.broadcasted_iota(jnp.int32, (1, LANES), 1) < 64
    tgt = jnp.concatenate([tgt_ref[...], tgt_ref[...]], axis=1)
    targets = jnp.concatenate(
        [jnp.where(half, tgt[2 * y:2 * y + 1], tgt[2 * y + 1:2 * y + 2]) for y in range(NY)], axis=1
    )

    def row_ids(i):
        return i * tile + lax.broadcasted_iota(jnp.int32, (tile, TOK), 0)

    def hot_tile(i, carry):
        at = pl.ds(pl.multiple_of(i * tile, tile), tile)
        ids = row_ids(i)
        ids = jnp.where(ids < VOC, ids, -2 * V_ALL)
        hot[at, :] = (ids + vocab_start == targets).astype(F32).astype(BF16)
        hotp[at, :] = (ids + other_start == targets).astype(F32).astype(BF16)
        return carry


    def rows_product(part, xs, mine, right, out, add):
        rows = PART_ROWS[part]
        ref, at = (wt, part_at[part]) if mine else (wtp, PART_AT[part])

        def body(i, carry):
            xat = pl.ds(i * xs, xs)
            left = ref[xat, :, pl.ds(at, rows), :].reshape(xs * NZ * rows, VPAD)
            t = jnp.dot(left, right[...], preferred_element_type=F32).reshape(xs, NZ * rows, TOK)
            if add:
                t = t + out[xat].astype(F32)
            out[xat] = t.astype(out.dtype)
            return carry

        lax.fori_loop(0, NX // xs, body, 0)

    def product(mine, right, outs, add):
        for part, xs in ((0, 2), (1, 2), (2, 4)):
            rows_product(part, xs, mine, right, outs[part], add)

    for j in (1, 3, 2):
        for p in (2, 0, 1):
            stage2[p][j - 1].wait()
            stage3[p, j] = start(ag_last(p, j))
            if p < 2:
                forward(p, j, 0)
    sq = sum_start(sum_end(sq, sqx), sqy, "y", sq_send, sq_recv, 2)
    lax.fori_loop(0, D // LANES // 4, gain_rows, 0)
    lax.fori_loop(0, VPAD // tile, hot_tile, 0)
    product(True, hot, (a0, a1, a2), False)

    wait(sq)
    mean_sq = jnp.concatenate([jnp.sum(sqy[y], axis=0, keepdims=True) for y in range(NY)], axis=0) / D
    invs[0:NY, :] = lax.rsqrt(mean_sq + EPSILON)

    def pass_on(j):
        for k in (1, 3, 2):
            stage3[0, j][k - 1].wait()
            forward(0, j, k)
        if j > 0:
            for jj in (0, 1, 3, 2):
                stage3[1, jj][j - 1].wait()
                forward(1, jj, j)

    def logits(j, first):
        wait(stage3[2, j])
        for k in range(4):
            forwards[0, j, k].wait()
            forwards[1, k, j].wait()
        xb = back("x", j)

        def normalize(z, carry):
            rows = pl.ds(pl.multiple_of(z * BLK, BLK), BLK)
            gain = gainb[pl.ds(pl.multiple_of((xb * NZ + z) * BLK, BLK), BLK), :]
            for y in range(NY):
                h = g[y, xb, z].astype(F32)
                n[rows, y * LANES:(y + 1) * LANES] = (h * invs[y:y + 1, :] * gain).astype(BF16)
            return carry

        lax.fori_loop(0, NZ, normalize, 0)
        t = jnp.dot(w[:, pl.ds(pl.multiple_of(xb * cut, LANES), cut)], n[...], preferred_element_type=F32)
        if first:
            acc[0:VOC, :] = t
        else:
            acc[0:VOC, :] += t

    pass_on(0)
    pass_on(1)
    logits(0, True)
    pass_on(3)
    logits(1, False)
    pass_on(2)
    far = pl.multiple_of(80 * other, 16)
    wt_copies = start([
        remote(wt.at[:, :, pl.ds(far, 64), :], wtp.at[:, :, pl.ds(0, 64), :], wt_send.at[0], wt_recv.at[0], partner),
        remote(wt.at[:, :, pl.ds(64, 16), :], wtp.at[:, :, pl.ds(64, 16), :], wt_send.at[1], wt_recv.at[1], partner),
    ])
    logits(3, False)
    logits(2, False)

    def fold(v):
        return jnp.sum(v.reshape(tile // 8, 8, TOK), axis=0)

    def softmax_tile(i, carry):
        tot, pick, dots = carry
        at = pl.ds(pl.multiple_of(i * tile, tile), tile)
        ids = row_ids(i)
        valid = ids < VOC
        raw = acc[at, :]
        th = jnp.tanh(raw * (1.0 / SOFTCAP))
        e = jnp.where(valid, jnp.exp(SOFTCAP * th), 0.0)
        at_target = jnp.logical_and(ids + vocab_start == targets, valid)
        term = jnp.where(jnp.logical_or(at_target, jnp.logical_not(valid)), 0.0, e * (1.0 - th * th)).astype(BF16)
        dl[at, :] = term
        term = term.astype(F32)
        return (
            tot + fold(e),
            pick + fold(jnp.where(at_target, raw, 0.0)),
            dots + fold(jnp.where(term == 0.0, 0.0, term * raw)),
        )

    zero = jnp.zeros((8, TOK), F32)
    carry = (zero, zero, zero)
    dl_copies = []
    for q in range(4):
        carry = lax.fori_loop(2 * q, 2 * q + 2, softmax_tile, carry)
        at = pl.ds(q * 2 * tile, 2 * tile)
        dl_copies += start([remote(dl.at[at, :], dlp.at[at, :], dl_send.at[q], dl_recv.at[q], partner)])

    def to_rows(v):
        v = jnp.sum(v, axis=0, keepdims=True)
        return [v[:, y * LANES:(y + 1) * LANES] for y in range(NY)]

    value = jnp.concatenate(
        to_rows(carry[0]) + to_rows(carry[1]) + to_rows(carry[2]) + [jnp.zeros((NY, LANES), F32)], axis=0
    )
    sums = sum_start(value, arz, "z", ar_send, ar_recv, 0)
    product(True, dl, (u0, u1, u2), False)
    sums = sum_start(sum_end(sums, arz), arx, "x", ar_send, ar_recv, 1)
    wait(wt_copies)
    product(False, hotp, (a0, a1, a2), True)
    sums = sum_start(sum_end(sums, arx), ary, "y", ar_send, ar_recv, 2)
    wait(dl_copies)
    product(False, dlp, (u0, u1, u2), True)
    sums = sum_start(sum_end(sums, ary), arc, "c", ar_send, ar_recv, 3)
    value = sum_end(sums, arc)

    exp_total = value[0:NY]
    target_raw = value[NY:2 * NY]
    dots = value[2 * NY:3 * NY]
    target_th = jnp.tanh(target_raw * (1.0 / SOFTCAP))
    target_capped = SOFTCAP * target_th
    logp = target_capped - jnp.log(exp_total)

    lane = lax.broadcasted_iota(jnp.int32, (GROUPS, LANES), 1)
    group = lax.broadcasted_iota(jnp.int32, (GROUPS, LANES), 0)
    own_half = (lane // 64) == (group % 2)
    seg = jnp.where(own_half, jnp.concatenate([seg_ref[...], seg_ref[...]], axis=1), -1)
    logp = jnp.concatenate([logp[r // 2:r // 2 + 1] for r in range(GROUPS)], axis=0)
    pairing = pair_ref[...]
    ref_logp = ref_ref[...]
    members, counts, adjusted = [], [], []
    for s in range(GROUPS):
        member = (seg == s).astype(F32)
        count = jnp.sum(member, axis=1, keepdims=True)
        members.append(member)
        counts.append(count)
        adjusted.append(jnp.sum(member * logp, axis=1, keepdims=True) / count - ref_logp[:, s:s + 1])
    margins, pulls, hots = [], [], []
    loss = jnp.zeros((GROUPS, 1), F32)
    for k in range(PAIRS):
        signs = [
            (pairing[:, 2 * k:2 * k + 1] == s).astype(F32) - (pairing[:, 2 * k + 1:2 * k + 2] == s).astype(F32)
            for s in range(GROUPS)
        ]
        margin = DPO_BETA * sum(sign * a for sign, a in zip(signs, adjusted))
        loss = loss + jnp.maximum(-margin, 0.0) + jnp.log1p(jnp.exp(-jnp.abs(margin)))
        hots.append(signs)
        margins.append(margin)
        pulls.append(-jax.nn.sigmoid(-margin) * (LOSS_SCALE / (GROUPS * PAIRS)))
    weight_rows = jnp.zeros((GROUPS, LANES), F32)
    for s in range(GROUPS):
        pull = DPO_BETA * sum(hots[k][s] * pulls[k] for k in range(PAIRS)) / counts[s]
        weight_rows = weight_rows + members[s] * pull
    token_weight = jnp.concatenate(
        [weight_rows[2 * y:2 * y + 1] + weight_rows[2 * y + 1:2 * y + 2] for y in range(NY)], axis=0
    )
    inv_total = 1.0 / exp_total
    at_target = token_weight * (1.0 - jnp.exp(target_capped) * inv_total) * (1.0 - target_th * target_th)
    elsewhere = -token_weight * inv_total
    coef[0:NY, :] = at_target
    coef[NY:2 * NY, :] = elsewhere
    dotb[0:NY, :] = jnp.where(at_target == 0.0, 0.0, at_target * target_raw) + elsewhere * dots

    s_bufs, r1, t1, r2 = (s0, s1, s2), (r01, r11, r21), (t01, t11, t21), (r02, r12, r22)
    t2, r3 = (t02, t12, t22), (r03, r13, r23)
    u_bufs, a_bufs = (u0, u1, u2), (a0, a1, a2)

    def blend(part, y, xb):
        rows = PART_ROWS[part]
        at = pl.ds(pl.multiple_of(y * LANES, LANES), LANES)
        v = coef[pl.ds(y, 1), :] * a_bufs[part][xb, :, at].astype(F32)
        v = v + coef[pl.ds(NY + y, 1), :] * u_bufs[part][xb, :, at]
        return v.astype(BF16).reshape(NZ, rows, LANES)

    def blend_part(part, j):
        def body(i, carry):
            if part == 0:
                s0[i, ahead("x", j)] = blend(0, i, ahead("x", j))
            elif part == 1:
                s1[i, ahead("y", j)] = blend(1, ahead("y", j), i)
            else:
                s2[ahead("x", j), :, i] = blend(2, i, ahead("x", j))
            return carry

        lax.fori_loop(0, 4, body, 0)

    def scatter1(part, j):
        first, second, _ = RS_ORDER[part]
        to2 = ahead(second, j)
        copies = []
        for k in range(1, SIZE[first]):
            to1 = ahead(first, k)
            src = s2.at[to2, to1] if part == 2 else s_bufs[part].at[to1, to2]
            copies.append(
                remote(src, r1[part].at[me[first], to2], rs1_send.at[part, j, k], rs1_recv.at[part, j, k],
                       device(first, k))
            )
        return start(copies)

    def gather1(part, j):
        first, second, _ = RS_ORDER[part]
        wait(scat1[part, j])
        to2 = ahead(second, j)
        own = s2.at[to2, me["z"]] if part == 2 else s_bufs[part].at[me[first], to2]
        return [own] + [r1[part].at[back(first, k), to2] for k in range(1, SIZE[first])]

    def add_up(refs, out):
        v = refs[0][...].astype(F32)
        for r in refs[1:]:
            v = v + r[...].astype(F32)
        out[...] = v.astype(BF16)

    scat1, scat2, scat3 = {}, {}, {}
    for j in (2, 1, 3, 0):
        for part in (2, 0, 1):
            blend_part(part, j)
            scat1[part, j] = scatter1(part, j)

    for j in (2, 1, 3, 0):
        for part in (2, 1, 0):
            second = RS_ORDER[part][1]
            to2 = ahead(second, j)
            piece = t1[part].at[to2]
            add_up(gather1(part, j), piece)
            if j > 0:
                scat2[part, j] = remote(
                    piece, r2[part].at[me[second]], rs2_send.at[part, j], rs2_recv.at[part, j], device(second, j)
                )
                scat2[part, j].start()

    for part in (1, 0, 2):
        second, third = RS_ORDER[part][1:]
        refs = [t1[part].at[me[second]]]
        for j in (2, 1, 3):
            scat2[part, j].wait()
            refs.append(r2[part].at[back(second, j)])
        add_up(refs, t2[part])
        scat3[part] = start([
            remote(t2[part].at[ahead(third, k)], r3[part].at[me[third]], rs3_send.at[part, k], rs3_recv.at[part, k],
                   device(third, k))
            for k in range(1, SIZE[third])
        ])

    col = lax.broadcasted_iota(jnp.int32, (GROUPS, LANES), 1)
    mbuf[...] = sum(jnp.where(col == k, margins[k], 0.0) for k in range(PAIRS))
    mar_ref[...] = mbuf[pl.ds(grp, 1), :][:, 0:PAIRS]
    loss_ref[...] = jnp.sum(loss, axis=0, keepdims=True) * (1.0 / (GROUPS * PAIRS))

    for part in range(3):
        third = RS_ORDER[part][2]
        wait(scat3[part])
        v = t2[part][me[third]].astype(F32)
        for k in range(1, SIZE[third]):
            v = v + r3[part][back(third, k)].astype(F32)
        fbuf[pl.ds(part_at[part], PART_ROWS[part]), :] = v
    mine = fbuf.at[pl.ds(own_at, 64), :]
    swap = remote(mine, mine, fin_send, fin_recv, partner)
    swap.start()
    swap.wait()

    own_inv = invs[pl.ds(me["y"], 1), :]
    own_dot = dotb[pl.ds(me["y"], 1), :]
    own_gain = gainb[pl.ds(pl.multiple_of(sec * BLK, BLK), BLK), :]
    own_hidden = g[me["y"], me["x"], me["z"]].astype(F32)
    result = own_gain * own_inv * fbuf[...] - own_hidden * (own_dot * own_inv * own_inv * (1.0 / D))
    result = jnp.concatenate([result, jnp.zeros((2 * LANES - BLK, LANES), F32)], axis=0)
    flipped = jnp.transpose(result)
    out_ref[...] = jnp.where(core == 0, flipped[0:64, 0:BLK], flipped[64:128, 0:BLK])


def per_device(hidden, norm_gain, weight, targets, segment_ids, pairing, ref_logp):
    vmem = pl.BlockSpec(memory_space=pltpu.VMEM)
    hbm = pl.BlockSpec(memory_space=pl.ANY)
    dma = pltpu.SemaphoreType.DMA
    V = pltpu.VMEM
    grad, margins, loss = pl.pallas_call(
        kernel,
        out_shape=(
            jax.ShapeDtypeStruct((64, BLK), F32),
            jax.ShapeDtypeStruct((1, PAIRS), F32),
            jax.ShapeDtypeStruct((1, 1), F32),
        ),
        in_specs=[hbm] * 7,
        out_specs=(vmem, vmem, vmem),
        scratch_shapes=[
            V((D // LANES, LANES), F32),
            V((GROUPS, 64), jnp.int32),
            V((GROUPS, 64), jnp.int32),
            V((GROUPS, GROUPS), jnp.int32),
            V((GROUPS, GROUPS), F32),
            V((VOC, D), BF16),
            V((NX, NZ, BLK, VPAD), BF16),
            V((NX, NZ, 80, VPAD), BF16),
            V((NY, NX, NZ, BLK, LANES), BF16),
            V((NZ * BLK, TOK), BF16),
            V((VPAD, TOK), F32),
            V((VPAD, TOK), BF16),
            V((VPAD, TOK), BF16),
            V((VPAD, TOK), BF16),
            V((VPAD, TOK), BF16),
            V((D, LANES), F32),
            V((2, 64, BLK), BF16),
            V((8, LANES), F32),
            V((NX, NZ * 32, TOK), F32),
            V((NX, NZ * 32, TOK), F32),
            V((NX, NZ * 16, TOK), F32),
            V((NX, NZ * 32, TOK), BF16),
            V((NX, NZ * 32, TOK), BF16),
            V((NX, NZ * 16, TOK), BF16),
            V((NY, NX, NZ, 32, LANES), BF16),
            V((NX, NY, NZ, 32, LANES), BF16),
            V((NX, NZ, NY, 16, LANES), BF16),
            V((NY, NX, NZ, 32, LANES), BF16),
            V((NX, NY, NZ, 32, LANES), BF16),
            V((NZ, NX, NY, 16, LANES), BF16),
            V((NX, NZ, 32, LANES), BF16),
            V((NY, NZ, 32, LANES), BF16),
            V((NX, NY, 16, LANES), BF16),
            V((NX, NZ, 32, LANES), BF16),
            V((NY, NZ, 32, LANES), BF16),
            V((NX, NY, 16, LANES), BF16),
            V((NZ, 32, LANES), BF16),
            V((NZ, 32, LANES), BF16),
            V((NY, 16, LANES), BF16),
            V((NZ, 32, LANES), BF16),
            V((NZ, 32, LANES), BF16),
            V((NY, 16, LANES), BF16),
            V((BLK, LANES), F32),
            V((NZ, 16, LANES), F32),
            V((NX, 16, LANES), F32),
            V((NY, 16, LANES), F32),
            V((2, 16, LANES), F32),
            V((NZ, 8, LANES), F32),
            V((NX, 8, LANES), F32),
            V((NY, 8, LANES), F32),
            V((8, LANES), F32),
            V((8, LANES), F32),
            V((8, LANES), F32),
            dma((6,)),
            dma((NX,)),
            dma, dma,
            dma((2, NZ)), dma((2, NZ)),
            dma((3, 4)), dma((3, 4)),
            dma((3, 4, NZ)), dma((3, 4, NZ)),
            dma((2, 4, 4)), dma((2, 4, 4)),
            dma((2,)), dma((2,)),
            dma((4,)), dma((4,)),
            dma((4, NZ)), dma((4, NZ)),
            dma((3, NZ)), dma((3, NZ)),
            dma((3, 4, NZ)), dma((3, 4, NZ)),
            dma((3, 4)), dma((3, 4)),
            dma((3, NZ)), dma((3, NZ)),
            dma, dma,
        ],
        compiler_params=pltpu.CompilerParams(
            collective_id=0, has_side_effects=True, vmem_limit_bytes=62 * 2**20
        ),
        name="dpo_output_layer",
    )(
        hidden,
        norm_gain.reshape(D // LANES, LANES),
        weight,
        targets,
        segment_ids,
        pairing,
        ref_logp,
    )
    return (grad, margins, loss.reshape(()))


def solution(mesh):
    in_specs = (P("dp", "section"), P(), P(("section", "dp"), None), P(), P(), P(), P())
    out_specs = (P("dp", "section"), P("dp", None), P())
    return jax.shard_map(
        per_device, mesh=mesh, in_specs=in_specs, out_specs=out_specs, check_vma=False
    )
```

time: 630 us -> 93.9 us (0.15)
  the two profiles are of different devices: /device:TPU:8 before, /device:TPU:1 now
where the time goes in v2:
time: 93.9 us; the launch traced here: 93.7 us
  Pallas kernels  88.8 us (95%)
  local copies, waits for them, and re-layouts  2.59 us (3%)
  between operations  2.33 us (2%)
    pallas_call x1, Pallas kernels, per_device(): pl.pallas_call(kernel, out_shape=(jax.ShapeDtypeStruct((64, BLK), F32), j...  88.8 us
    unnamed x2, local copies, waits for them, and re-layouts  2.59 us

profile of v2, /device:TPU:1, one launch (start us, length us, event | category | flops | bytes accessed | tf_op | source)
XLA Modules:
  0.0 93.7 jit_solution(9567155321517762189)
XLA Ops:
  0.6 88.8 %dpo_output_layer.1 = (f32[64,144]{1,0:T(8,128)}, f32[1,4]{1,0:T(1,128)}, f32[1,1]{1,0:T(1,128)}) custom-call(bf16[64,144]{1,0:T(8,128)(2,1)} %hid_hbm.1, f32[36,128]{1,0:T(8,128)} %bitcast.2, bf16[1000,4608]{1,0:T(8,128)(2,1)} %w_hbm.1, s32[8,64]{1,0:T(8,128)} %tgt_hbm.1, s32[8,64]{1,0:T(8,128)} %seg_hbm.1, s32[8,8]{1,0:T(8,128)} %pair_hbm.1, f32[8,8]{1,0:T(8,128)} %ref_hbm.1), custom_call_target="tpu_custom_call" | custom-call | tf_op jit(solution)/shard_map/dpo_output_layer/pallas_call | solution.py:515
  89.5 1.5 %copy.13 = f32[64,144]{1,0:T(8,128)} copy(f32[64,144]{1,0:T(8,128)} %get-tuple-element.12) | data formatting | bytes 73728
  90.9 1.1 %copy.14 = f32[1,4]{1,0:T(1,128)} copy(f32[1,4]{1,0:T(1,128)} %get-tuple-element.13) | data formatting | bytes 32

commit v3 on v2

--- a/solution.py
+++ b/solution.py
@@ -255,7 +255,6 @@
     sq = sum_start(sum_end(sq, sqx), sqy, "y", sq_send, sq_recv, 2)
     lax.fori_loop(0, D // LANES // 4, gain_rows, 0)
     lax.fori_loop(0, VPAD // tile, hot_tile, 0)
-    product(True, hot, (a0, a1, a2), False)
 
     wait(sq)
     mean_sq = jnp.concatenate([jnp.sum(sqy[y], axis=0, keepdims=True) for y in range(NY)], axis=0) / D
@@ -344,6 +343,7 @@
     )
     sums = sum_start(value, arz, "z", ar_send, ar_recv, 0)
     product(True, dl, (u0, u1, u2), False)
+    product(True, hot, (a0, a1, a2), False)
     sums = sum_start(sum_end(sums, arz), arx, "x", ar_send, ar_recv, 1)
     wait(wt_copies)
     product(False, hotp, (a0, a1, a2), True)
@@ -456,7 +456,7 @@
             scat1[part, j] = scatter1(part, j)
 
     for j in (2, 1, 3, 0):
-        for part in (2, 1, 0):
+        for part in (0, 1, 2):
             second = RS_ORDER[part][1]
             to2 = ahead(second, j)
             piece = t1[part].at[to2]

time: 93.9 us -> 97.1 us (1.034)
  Pallas kernels: 88.8 us -> 92 us
    pallas_call x1, Pallas kernels: 88.8 us -> 92 us  [per_device(): pl.pallas_call(kernel, out_shape=(jax.ShapeDtypeStruct((64, BLK), F32), j...]
where the time goes in v3:
time: 97.1 us; the launch traced here: 96.9 us
  Pallas kernels  92 us (95%)
  local copies, waits for them, and re-layouts  2.59 us (3%)
  between operations  2.33 us (2%)
    pallas_call x1, Pallas kernels, per_device(): pl.pallas_call(kernel, out_shape=(jax.ShapeDtypeStruct((64, BLK), F32), j...  92 us
    unnamed x2, local copies, waits for them, and re-layouts  2.59 us

profile of v3, /device:TPU:1, one launch (start us, length us, event | category | flops | bytes accessed | tf_op | source)
XLA Modules:
  0.0 96.9 jit_solution(6969915161528760057)
XLA Ops:
  0.6 92.0 %dpo_output_layer.1 = (f32[64,144]{1,0:T(8,128)}, f32[1,4]{1,0:T(1,128)}, f32[1,1]{1,0:T(1,128)}) custom-call(bf16[64,144]{1,0:T(8,128)(2,1)} %hid_hbm.1, f32[36,128]{1,0:T(8,128)} %bitcast.2, bf16[1000,4608]{1,0:T(8,128)(2,1)} %w_hbm.1, s32[8,64]{1,0:T(8,128)} %tgt_hbm.1, s32[8,64]{1,0:T(8,128)} %seg_hbm.1, s32[8,8]{1,0:T(8,128)} %pair_hbm.1, f32[8,8]{1,0:T(8,128)} %ref_hbm.1), custom_call_target="tpu_custom_call" | custom-call | tf_op jit(solution)/shard_map/dpo_output_layer/pallas_call | solution.py:515
  92.6 1.5 %copy.13 = f32[64,144]{1,0:T(8,128)} copy(f32[64,144]{1,0:T(8,128)} %get-tuple-element.12) | data formatting | bytes 73728
  94.1 1.1 %copy.14 = f32[1,4]{1,0:T(1,128)} copy(f32[1,4]{1,0:T(1,128)} %get-tuple-element.13) | data formatting | bytes 32
